TPU v7x, 32 devices: a whole 2x2x4 slice. The times are simulated.
32 devices in a mesh: ctx: 16 (over z, y, core), head: 2 (over x).
Axes of the slice: x: 2, y: 2, z: 4, core: 2. Of those that a mesh axis runs over, the one named last changes fastest.
Arguments:
- queries: bfloat16 [8192, 4096], P(('ctx', 'head')), may hold values from -12 to 12
- keys: bfloat16 [8192, 1024], P(('ctx', 'head')), may hold values from -12 to 12
- values: bfloat16 [8192, 1024], P(('ctx', 'head')), may hold values from -6 to 6
- doc_lengths: int32 [4], replicated, may hold values from 1 to 4096, 8192 in all
- piece_owner: int32 [16, 16], P('ctx'), may hold values from 0 to 15, each once within a row
Outputs:
- owned: bfloat16 [8192, 4096], P('ctx', 'head')
Inputs may be any that keep to these rules, and one draw needn't show every extreme that they name: Each row of piece_owner is a permutation of 0 .. 15. doc_lengths sum to 8192, and the largest equals 4096.
All inputs are finite; a program needn't handle non-finite values.
Results may differ from a plain program's by a relative error of at most 0.0033.
Values may be sent and summed in bfloat16 or wider, within the bound.
No kernel may reach another device: no remote copies, remote signals or barrier semaphores. Data moves between devices by JAX's collectives and lax.ppermute only.
A program may use at most 128 MiB of HBM per device.

v0:
```python
import math

import jax
import jax.numpy as jnp
from jax import lax
from jax.experimental import pallas as pl
from jax.experimental.pallas import tpu as pltpu
from jax.sharding import Mesh
from jax.sharding import PartitionSpec as P

HD = 128
QPK = 4
MOST = 4096
Q_ROWS = 256
K_LONG = 1024
K_SHORT = 256
MASKED = -1e30
SCALE = math.log2(math.e) / math.sqrt(HD)
VMEM = 32 * 1024 * 1024


def doc_start(place, ends):
    start = jnp.zeros_like(place)
    for end in ends:
        start = jnp.maximum(start, jnp.where(end <= place, end, 0))
    return start


class Block:
    def __init__(self, ends, first_row, base, window, turned, values, qs, top, total):
        self.ends = ends
        self.first_row, self.base, self.window = first_row, base, window
        self.turned, self.values, self.qs, self.top, self.total = turned, values, qs, top, total
        self.first_start = doc_start(first_row, self.ends) - base
        self.last_start = doc_start(first_row + Q_ROWS - 1, self.ends) - base

    def load(self, q_ref):
        for head in range(QPK):
            scaled = q_ref[:, head * HD : (head + 1) * HD].astype(jnp.float32) * SCALE
            high = scaled.astype(jnp.bfloat16)
            rows = slice(head * Q_ROWS, (head + 1) * Q_ROWS)
            self.qs[rows, :HD] = high
            self.qs[rows, HD:] = (scaled - high.astype(jnp.float32)).astype(jnp.bfloat16)

    def run(self, at, size, masked):
        at = pl.multiple_of(at, K_SHORT)
        keys = self.turned[:, pl.ds(at, size)]
        keys = jnp.concatenate([keys, keys], axis=0)
        values = self.values[pl.ds(at, size), :]
        values = jnp.concatenate([values, jnp.ones_like(values)], axis=1)
        if masked:
            shape = (Q_ROWS, size)
            row = self.first_row + lax.broadcasted_iota(jnp.int32, (Q_ROWS, 1), 0)
            place = self.base + at + lax.broadcasted_iota(jnp.int32, shape, 1)
            live = (place <= row) & (place >= doc_start(row, self.ends))

        def score(head):
            rows = slice(head * Q_ROWS, (head + 1) * Q_ROWS)
            return jnp.dot(self.qs[rows], keys, preferred_element_type=jnp.float32)

        scores = score(0)
        for head in range(QPK):
            rows = slice(head * Q_ROWS, (head + 1) * Q_ROWS)
            upcoming = score(head + 1) if head + 1 < QPK else None
            if masked:
                scores = jnp.where(live, scores, MASKED)
            old_top = self.top[rows]
            new_top = jnp.maximum(old_top, jnp.max(scores, axis=1, keepdims=True))
            weights = jnp.exp2(scores - jnp.concatenate([new_top] * (size // HD), axis=1))
            part = jnp.dot(weights.astype(jnp.bfloat16), values, preferred_element_type=jnp.float32)
            factor = jnp.exp2(old_top - new_top)
            self.total[rows] = self.total[rows] * jnp.concatenate([factor, factor], axis=1) + part
            self.top[rows] = new_top
            scores = upcoming

    def cover(self, high, long):
        low = jnp.clip(self.first_start, 0, self.window) // K_SHORT * K_SHORT
        plain = (jnp.clip(self.last_start, 0, self.window) + K_SHORT - 1) // K_SHORT * K_SHORT
        for size, masked, until in ((long, False, plain), (long, True, low), (K_SHORT, True, low)):
            count = jnp.maximum(high - until, 0) // size
            lax.fori_loop(
                0,
                count,
                lambda step, _, high=high, size=size, masked=masked: self.run(high - (step + 1) * size, size, masked),
                None,
            )
            high = high - count * size

    def deliver(self, step, owner, stage, out, sems):
        piece = stage.shape[1]
        slots = Q_ROWS // piece
        for head in range(QPK):
            rows = slice(head * Q_ROWS, (head + 1) * Q_ROWS)
            done = (self.total[rows, :HD] / self.total[rows, HD:]).astype(jnp.bfloat16)
            for part in range(slots):
                stage[step * slots + part, :, head * HD : (head + 1) * HD] = done[part * piece : (part + 1) * piece]
        lax.fori_loop(0, slots, lambda part, _: sent(step * slots + part, owner, stage, out, sems).start(), None)


def sent(slot, owner, stage, out, sems):
    return pltpu.make_async_copy(stage.at[slot], out.at[owner[slot // out.shape[0], slot % out.shape[0]], slot // out.shape[0]], sems.at[slot])


def arrange(refs, turned, values):
    tokens = refs[0].shape[0]
    for index, ref in enumerate(refs):
        values[index * tokens : (index + 1) * tokens] = ref[:, :HD]

        def turn(tile, carry, ref=ref, index=index):
            rows = pl.ds(pl.multiple_of(tile * HD, HD), HD)
            turned[:, pl.ds(pl.multiple_of(index * tokens + tile * HD, HD), HD)] = ref[rows, HD:].T
            return carry

        lax.fori_loop(0, tokens // HD, turn, 0)


def keep(step, slot, top, total, tops, totals, kept, back):
    pairs = ((top.at[slot], tops.at[step]), (total.at[slot], totals.at[step]))
    if back:
        pairs = [pair[::-1] for pair in pairs]
    return [pltpu.make_async_copy(*pair, kept.at[slot, index]) for index, pair in enumerate(pairs)]


def far_blocks(place, ends, tokens):
    count = 0
    for step in range(tokens // Q_ROWS):
        count += (doc_start(place + step * Q_ROWS, ends) < place - tokens).astype(jnp.int32)
    return count


def ends_of(lengths):
    ends = [lengths[0]]
    for doc in range(1, lengths.shape[0]):
        ends.append(ends[-1] + lengths[doc])
    return ends


def near_kernel(at, lengths, owner, q_ref, own, near, out, tops, totals, turned, values, qs, top, total, stage, sems, kept):
    tokens = own.shape[0]
    step = pl.program_id(0)
    slot = lax.rem(step, 2)
    place = at[0]
    ends = ends_of(lengths)
    needed = far_blocks(place, ends, tokens)
    slots = Q_ROWS // stage.shape[1]

    @pl.when(step == 0)
    def _():
        arrange((near, own), turned, values)

    @pl.when((step >= 2) & (step - 2 < needed))
    def _():
        for copy in keep(step - 2, slot, top, total, tops, totals, kept, False):
            copy.wait()

    first_row = place + step * Q_ROWS
    block = Block(ends, first_row, place - tokens, 2 * tokens, turned, values, qs, top.at[slot], total.at[slot])
    block.load(q_ref)
    top[slot] = jnp.full(top.shape[1:], MASKED, jnp.float32)
    total[slot] = jnp.zeros(total.shape[1:], jnp.float32)
    long = min(K_LONG, tokens)
    high = tokens + (step + 1) * Q_ROWS - long
    block.run(high, long, True)
    block.cover(high, long)

    @pl.when(step >= needed)
    def _():
        block.deliver(step, owner, stage, out, sems)

    @pl.when(step < needed)
    def _():
        for copy in keep(step, slot, top, total, tops, totals, kept, False):
            copy.start()

    blocks = tokens // Q_ROWS

    @pl.when(step == blocks - 1)
    def _():
        for last in range(max(blocks - 2, 0), blocks):

            @pl.when(last < needed)
            def _(last=last):
                for copy in keep(last, last % 2, top, total, tops, totals, kept, False):
                    copy.wait()

        finish(needed * slots, blocks * slots, owner, stage, out, sems)


def finish(first, last, owner, stage, out, sems):
    lax.fori_loop(first, last, lambda slot, _: sent(slot, owner, stage, out, sems).wait(), None)


def far_kernel(at, lengths, owner, q_rows, tops, totals, begun, *refs):
    far, (out, held, fetched, turned, values, qs, top, total, stage, sems, kept, brought) = refs[:-12], refs[-12:]
    del begun
    tokens = q_rows.shape[0]
    window = tokens * len(far)
    place = at[0]
    ends = ends_of(lengths)
    needed = far_blocks(place, ends, tokens)

    def coming(step, slot):
        copies = keep(step, slot, top, total, tops, totals, kept, True)
        rows = pl.ds(pl.multiple_of(step * Q_ROWS, Q_ROWS), Q_ROWS)
        return copies + [pltpu.make_async_copy(q_rows.at[rows], held.at[slot], kept.at[slot, 2])]

    @pl.when(needed > 0)
    def _():
        whole = [pltpu.make_async_copy(ref, fetched.at[index], brought.at[index]) for index, ref in enumerate(far[::-1])]
        for copy in whole + coming(0, 0):
            copy.start()
        for copy in whole:
            copy.wait()
        arrange([fetched.at[index] for index in range(len(far))], turned, values)

    def one(step, carry):
        slot = lax.rem(step, 2)

        @pl.when(step + 1 < needed)
        def _():
            for copy in coming(step + 1, 1 - slot):
                copy.start()

        first_row = place + step * Q_ROWS
        block = Block(ends, first_row, place - tokens - window, window, turned, values, qs, top.at[slot], total.at[slot])
        for copy in coming(step, slot):
            copy.wait()
        block.load(held.at[slot])
        block.cover(window, min(K_LONG, tokens))
        block.deliver(step, owner, stage, out, sems)
        return carry

    lax.fori_loop(0, needed, one, 0)
    finish(0, needed * (Q_ROWS // stage.shape[1]), owner, stage, out, sems)


def attend(at, lengths, owner, n_owner, piece, query_rows, own, steps_back):
    tokens, features = query_rows.shape
    blocks = tokens // Q_ROWS
    near, far = steps_back[0], steps_back[1:]
    rows = QPK * Q_ROWS
    any_spec = pl.BlockSpec(memory_space=pl.ANY)
    paired_spec = pl.BlockSpec(own.shape, lambda i, *_: (0, 0))
    out_shape = jax.ShapeDtypeStruct((n_owner, tokens // (n_owner * piece), piece, features), jnp.bfloat16)
    state_shapes = [
        jax.ShapeDtypeStruct((blocks, rows, HD), jnp.float32),
        jax.ShapeDtypeStruct((blocks, rows, 2 * HD), jnp.float32),
    ]

    def scratch(window):
        return [
            pltpu.VMEM((HD, window), jnp.bfloat16),
            pltpu.VMEM((window, HD), jnp.bfloat16),
            pltpu.VMEM((rows, 2 * HD), jnp.bfloat16),
            pltpu.VMEM((2, rows, HD), jnp.float32),
            pltpu.VMEM((2, rows, 2 * HD), jnp.float32),
            pltpu.VMEM((tokens // piece, piece, features), jnp.bfloat16),
            pltpu.SemaphoreType.DMA((tokens // piece,)),
            pltpu.SemaphoreType.DMA((2, 3)),
        ]

    begun, tops, totals = pl.pallas_call(
        near_kernel,
        grid_spec=pltpu.PrefetchScalarGridSpec(
            num_scalar_prefetch=3,
            grid=(blocks,),
            in_specs=[pl.BlockSpec((Q_ROWS, features), lambda i, *_: (i, 0)), paired_spec, paired_spec],
            out_specs=[any_spec] * 3,
            scratch_shapes=scratch(2 * tokens),
        ),
        out_shape=[out_shape, *state_shapes],
        compiler_params=pltpu.CompilerParams(vmem_limit_bytes=VMEM),
        cost_estimate=pl.CostEstimate(flops=20_000_000_000, bytes_accessed=1 << 23, transcendentals=0),
        name="attend_near",
    )(at, lengths, owner, query_rows, own, near)
    if not far:
        return begun
    return pl.pallas_call(
        far_kernel,
        grid_spec=pltpu.PrefetchScalarGridSpec(
            num_scalar_prefetch=3,
            grid=(),
            in_specs=[any_spec] * (4 + len(far)),
            out_specs=any_spec,
            scratch_shapes=[
                pltpu.VMEM((2, Q_ROWS, features), jnp.bfloat16),
                pltpu.VMEM((len(far),) + own.shape, jnp.bfloat16),
                *scratch(tokens * len(far)),
                pltpu.SemaphoreType.DMA((len(far),)),
            ],
        ),
        out_shape=out_shape,
        input_output_aliases={6: 0},
        compiler_params=pltpu.CompilerParams(vmem_limit_bytes=VMEM),
        cost_estimate=pl.CostEstimate(flops=5_000_000_000, bytes_accessed=1 << 23, transcendentals=0),
        name="attend_far",
    )(at, lengths, owner, query_rows, tops, totals, begun, *far)


def moved_blocks(arrays, out_shape, routes, name):
    def kernel(*refs):
        ins, out, sems = refs[: len(arrays)], refs[-2], refs[-1]
        copies = [
            pltpu.make_async_copy(ins[index].at[here], out.at[there], sems.at[number])
            for number, (index, here, there) in enumerate(routes)
        ]
        for copy in copies:
            copy.start()
        for copy in copies:
            copy.wait()

    any_spec = pl.BlockSpec(memory_space=pl.ANY)
    return pl.pallas_call(
        kernel,
        in_specs=[any_spec] * len(arrays),
        out_specs=any_spec,
        out_shape=jax.ShapeDtypeStruct(out_shape, arrays[0].dtype),
        scratch_shapes=[pltpu.SemaphoreType.DMA((len(routes),))],
        name=name,
    )(*arrays)


def dealt(arrays, n_head, group, name):
    heads = n_head * group
    tok = arrays[0].shape[0]
    widths = [array.shape[1] // heads for array in arrays]
    routes = []
    for index, width in enumerate(widths):
        left = sum(widths[:index])
        for local in range(group):
            for head in range(n_head):
                source = (head * group + local) * width
                there = (local * n_head + head, slice(None), slice(left, left + width))
                routes.append((index, (slice(None), slice(source, source + width)), there))
    return moved_blocks(arrays, (heads, tok, sum(widths)), routes, name)


def laid_out(received, planes, group):
    _, rows, features = received.shape
    if group == 1:
        return received.reshape(planes * rows, features)
    routes = [
        (
            0,
            (plane * group + local,),
            (slice(plane * rows, (plane + 1) * rows), slice(local * features, (local + 1) * features)),
        )
        for plane in range(planes)
        for local in range(group)
    ]
    return moved_blocks([received], (planes * rows, group * features), routes, "lay_out")


def solution(mesh):
    n_ctx, n_head = mesh.shape["ctx"], mesh.shape["head"]

    def run(queries, keys, values, doc_lengths, piece_owner):
        group = keys.shape[1] // (HD * n_head)
        planes = n_ctx // group
        grouped = Mesh(mesh.devices.reshape(planes, group, n_head), ("plane", "local", "head"))
        rows = P(("plane", "local", "head"), None)

        def exchanged(split):
            moved = lax.all_to_all(split, ("local", "head"), split_axis=0, concat_axis=0, tiled=True)
            return moved.reshape(-1, split.shape[-1])

        def per_device(queries, keys, values, doc_lengths, piece_owner):
            paired = dealt([values, keys], n_head, group, "deal_keys")
            own = exchanged(paired)
            tokens = own.shape[0]
            reach = (MOST - 1) // tokens + 1
            up = [(plane, plane + 1) for plane in range(planes - 1)]
            steps_back = []
            moving = own
            for _ in range(reach):
                moving = lax.ppermute(moving, "plane", up)
                steps_back.append(moving)
            owner = lax.all_gather(piece_owner, "local", axis=0, tiled=True)
            split = dealt([queries], n_head, group, "deal_queries")
            split, owner = lax.optimization_barrier((split, owner))
            query_rows = exchanged(split)
            at = (lax.axis_index("plane") * tokens).astype(jnp.int32)[None]
            piece = tokens // (group * n_ctx)
            ordered = attend(at, doc_lengths, owner, n_ctx, piece, query_rows, own, steps_back)
            ordered = ordered.reshape(n_ctx, group * piece, -1)
            received = lax.all_to_all(ordered, ("plane", "local"), split_axis=0, concat_axis=0, tiled=True)
            return laid_out(received, planes, group)

        return jax.shard_map(
            per_device,
            mesh=grouped,
            in_specs=(rows, rows, rows, P(), P(("plane", "local"), None)),
            out_specs=P(("plane", "local"), "head"),
            check_vma=False,
        )(queries, keys, values, doc_lengths, piece_owner)

    return run
```

profile of v0, /device:TPU:1, one launch (start us, length us, event | category | flops | bytes accessed | tf_op | source)
XLA Modules:
  0.0 316.6 jit_solution(6684678667641069183)
XLA Ops:
  0.0 33.0 %deal_keys.1 = bf16[8,256,256]{2,1,0:T(8,128)(2,1)} custom-call(bf16[256,1024]{1,0:T(8,128)(2,1)} %refs_0_.3, bf16[256,1024]{1,0:T(8,128)(2,1)} %refs_1_.1), custom_call_target="tpu_custom_call" | custom-call | tf_op jit(solution)/shard_map/deal_keys/pallas_call | solution.py:313
  33.0 5.2 %all-to-all-start.1 = ((bf16[8,256,256]{2,1,0:T(8,128)(2,1)}), bf16[8,256,256]{2,1,0:T(8,128)(2,1)S(1)}, u32[]{:S(2)}, u32[]{:S(2)}) async-start(bf16[8,256,256]{2,1,0:T(8,128)(2,1)} %deal_keys.1), calls=%async_computation.1 | async-start | bytes 2097152 | tf_op jit(solution)/shard_map/all_to_all | solution.py:364
  38.3 0.0 copy-start.1
  38.3 64.7 %deal_queries.1 = bf16[8,256,512]{2,1,0:T(8,128)(2,1)} custom-call(bf16[256,4096]{1,0:T(8,128)(2,1)} %refs_0_.2), custom_call_target="tpu_custom_call" | custom-call | tf_op jit(solution)/shard_map/deal_queries/pallas_call | solution.py:313
  103.0 0.0 copy-done.1
  103.0 5.0 %all-gather = s32[4,1,16]{2,1,0:T(1,128)S(1)} all-gather(s32[1,1,16]{2,1,0:T(1,128)S(1)} %bitcast.13), channel_id=1, replica_groups=mesh['plane'=4,'local'=4,'head'=2] {'local'}, dimensions={0}, use_global_device_ids=true | all-gather | bytes 320 | tf_op jit(solution)/shard_map/all_gather | solution.py:378
  107.9 0.0 copy-start
  107.9 0.0 all-to-all-done.1
  107.9 4.4 %all-to-all-start = ((bf16[8,256,512]{2,1,0:T(8,128)(2,1)}), bf16[8,256,512]{2,1,0:T(8,128)(2,1)S(1)}, u32[]{:S(2)}, u32[]{:S(2)}) async-start(bf16[8,256,512]{2,1,0:T(8,128)(2,1)} %deal_queries.1), calls=%async_computation | async-start | bytes 4194304 | tf_op jit(solution)/shard_map/all_to_all | solution.py:364
  112.3 4.2 %collective-permute-start = (bf16[2048,256]{1,0:T(8,128)(2,1)S(1)}, bf16[2048,256]{1,0:T(8,128)(2,1)}, u32[]{:S(2)}, u32[]{:S(2)}) collective-permute-start(bf16[2048,256]{1,0:T(8,128)(2,1)S(1)} %bitcast.9), channel_id=1, source_target_pairs={{0,8},{8,16},{16,24},{1,9},{9,17},{17,25},{2,10},{10,18},{18,26},{... | collective-permute-start | bytes 3145736 | tf_op jit(solution)/shard_map/ppermute | solution.py:376
  116.5 21.6 %collective-permute-done.near = bf16[2048,256]{1,0:T(8,128)(2,1)} collective-permute-done((bf16[2048,256]{1,0:T(8,128)(2,1)S(1)}, bf16[2048,256]{1,0:T(8,128)(2,1)}, u32[]{:S(2)}, u32[]{:S(2)}) %collective-permute-start) | collective-permute-done | bytes 1048608 | tf_op jit(solution)/shard_map/ppermute | solution.py:376
  138.1 5.2 %collective-permute-start.1 = (bf16[2048,256]{1,0:T(8,128)(2,1)}, bf16[2048,256]{1,0:T(8,128)(2,1)}, u32[]{:S(2)}, u32[]{:S(2)}) collective-permute-start(bf16[2048,256]{1,0:T(8,128)(2,1)} %collective-permute-done.near), channel_id=1, source_target_pairs={{0,8},{8,16},{16,24},{1,9},{9,17},{17,25},{2,10},{10,18},{18,26},{... | collective-permute-start | bytes 3145736 | tf_op jit(solution)/shard_map/ppermute | solution.py:376
  143.4 0.0 all-to-all-done
  143.4 0.0 copy-done
  143.4 26.6 %attend_near.1 = (bf16[16,4,32,512]{3,2,1,0:T(8,128)(2,1)S(1)}, f32[8,1024,128]{2,1,0:T(8,128)S(1)}, f32[8,1024,256]{2,1,0:T(8,128)S(1)}) custom-call(s32[1]{0:T(128)} %bitcast.at, s32[4]{0:T(128)S(1)} %copy-done, s32[4,16]{1,0:T(4,128)S(1)} %bitcast.11, bf16[2048,512]{1,0:T(8,128)(2,1)S(1)} %bitcast.6, bf16[2048,256]{1,0:T(8,128)(2,1)S(1)} %bitcast.10, ...), custom_call_target="tpu_custom_call" | custom-call | flops 20000000000 | bytes 8388608 | tf_op jit(solution)/shard_map/attend_near/pallas_call | solution.py:262
  169.9 0.0 collective-permute-done.1.refs_0_
  169.9 1.3 attend_far.1
  171.2 80.6 %all_to_all.15.refs_0_ = bf16[16,128,512]{2,1,0:T(8,128)(2,1)} all-to-all(bf16[16,128,512]{2,1,0:T(8,128)(2,1)S(1)} %bitcast.8), channel_id=1, replica_groups=mesh['plane'=4,'local'=4,'head'=2] {'plane','local'}, dimensions={0} | all-to-all | bytes 4194304 | tf_op jit(solution)/shard_map/all_to_all | solution.py:386
  251.8 64.8 %lay_out.1 = bf16[512,2048]{1,0:T(8,128)(2,1)} custom-call(bf16[16,128,512]{2,1,0:T(8,128)(2,1)} %all_to_all.15.refs_0_), custom_call_target="tpu_custom_call" | custom-call | tf_op jit(solution)/shard_map/lay_out/pallas_call | solution.py:313
Async XLA Ops:
  33.0 74.9 %all-to-all-start.1 = ((bf16[8,256,256]{2,1,0:T(8,128)(2,1)}), bf16[8,256,256]{2,1,0:T(8,128)(2,1)S(1)}, u32[]{:S(2)}, u32[]{:S(2)}) async-start(bf16[8,256,256]{2,1,0:T(8,128)(2,1)} %deal_keys.1), calls=%async_computation.1 | async-start | bytes 2097152 | tf_op jit(solution)/shard_map/all_to_all | solution.py:364
  38.3 64.7 %copy-start.1 = (s32[1,16]{1,0:T(1,128)S(1)}, s32[1,16]{1,0:T(1,128)}, u32[]{:S(2)}) copy-start(s32[1,16]{1,0:T(1,128)} %param.9) | copy-start | bytes 196
  107.9 35.4 %copy-start = (s32[4]{0:T(128)S(1)}, s32[4]{0:T(128)}, u32[]{:S(2)}) copy-start(s32[4]{0:T(128)} %lengths.3) | copy-start | bytes 52
  107.9 35.4 %all-to-all-start = ((bf16[8,256,512]{2,1,0:T(8,128)(2,1)}), bf16[8,256,512]{2,1,0:T(8,128)(2,1)S(1)}, u32[]{:S(2)}, u32[]{:S(2)}) async-start(bf16[8,256,512]{2,1,0:T(8,128)(2,1)} %deal_queries.1), calls=%async_computation | async-start | bytes 4194304 | tf_op jit(solution)/shard_map/all_to_all | solution.py:364
  112.3 25.8 %collective-permute-start = (bf16[2048,256]{1,0:T(8,128)(2,1)S(1)}, bf16[2048,256]{1,0:T(8,128)(2,1)}, u32[]{:S(2)}, u32[]{:S(2)}) collective-permute-start(bf16[2048,256]{1,0:T(8,128)(2,1)S(1)} %bitcast.9), channel_id=1, source_target_pairs={{0,8},{8,16},{16,24},{1,9},{9,17},{17,25},{2,10},{10,18},{18,26},{... | collective-permute-start | bytes 3145736 | tf_op jit(solution)/shard_map/ppermute | solution.py:376
  138.1 31.8 %collective-permute-start.1 = (bf16[2048,256]{1,0:T(8,128)(2,1)}, bf16[2048,256]{1,0:T(8,128)(2,1)}, u32[]{:S(2)}, u32[]{:S(2)}) collective-permute-start(bf16[2048,256]{1,0:T(8,128)(2,1)} %collective-permute-done.near), channel_id=1, source_target_pairs={{0,8},{8,16},{16,24},{1,9},{9,17},{17,25},{2,10},{10,18},{18,26},{... | collective-permute-start | bytes 3145736 | tf_op jit(solution)/shard_map/ppermute | solution.py:376
where the time goes:
time: 317 us
  Pallas kernels  190 us (60%)
  blocking collectives  85.6 us (27%)
  waiting for transfers between devices  21.6 us (7%)
  starting transfers between devices  19.1 us (6%)
    pallas_call x3, Pallas kernels, moved_blocks(): pl.pallas_call(kernel, in_specs=[any_spec] * len(arrays), out_specs=any_s...  162 us
    all_to_all x1, blocking collectives, per_device(): lax.all_to_all(ordered, ('plane', 'local'), split_axis=0, concat_axis=0,...  80.6 us
    pallas_call x1, Pallas kernels, attend(): pl.pallas_call(near_kernel, grid_spec=pltpu.PrefetchScalarGridSpec(num_sc...  26.6 us
    ppermute x2, waiting for transfers between devices, per_device(): moving = lax.ppermute(moving, 'plane', up)  21.6 us
    all_to_all x2, starting transfers between devices, exchanged(): lax.all_to_all(split, ('local', 'head'), split_axis=0, concat_axis=0, til...  9.65 us
    ppermute x2, starting transfers between devices, per_device(): moving = lax.ppermute(moving, 'plane', up)  9.4 us
  transfers between devices with their start and end apart: 4, of which 1 were waited for; matrix products, arithmetic and copies ran while one was open for 0% of the time, Pallas kernels for 29%

commit v1 on v0

--- a/solution.py
+++ b/solution.py
@@ -297,58 +297,50 @@
     )(at, lengths, owner, query_rows, tops, totals, begun, *far)
 
 
-def moved_blocks(arrays, out_shape, routes, name):
-    def kernel(*refs):
-        ins, out, sems = refs[: len(arrays)], refs[-2], refs[-1]
-        copies = [
-            pltpu.make_async_copy(ins[index].at[here], out.at[there], sems.at[number])
-            for number, (index, here, there) in enumerate(routes)
-        ]
-        for copy in copies:
-            copy.start()
-        for copy in copies:
-            copy.wait()
-
-    any_spec = pl.BlockSpec(memory_space=pl.ANY)
-    return pl.pallas_call(
-        kernel,
-        in_specs=[any_spec] * len(arrays),
-        out_specs=any_spec,
-        out_shape=jax.ShapeDtypeStruct(out_shape, arrays[0].dtype),
-        scratch_shapes=[pltpu.SemaphoreType.DMA((len(routes),))],
-        name=name,
-    )(*arrays)
-
-
 def dealt(arrays, n_head, group, name):
     heads = n_head * group
     tok = arrays[0].shape[0]
     widths = [array.shape[1] // heads for array in arrays]
-    routes = []
-    for index, width in enumerate(widths):
-        left = sum(widths[:index])
-        for local in range(group):
+    step_rows = max(tok // 4, 16)
+
+    def kernel(*refs):
+        out = refs[-1]
+        for index, width in enumerate(widths):
+            left = sum(widths[:index])
             for head in range(n_head):
-                source = (head * group + local) * width
-                there = (local * n_head + head, slice(None), slice(left, left + width))
-                routes.append((index, (slice(None), slice(source, source + width)), there))
-    return moved_blocks(arrays, (heads, tok, sum(widths)), routes, name)
+                for local in range(group):
+                    source = (head * group + local) * width
+                    out[local * n_head + head, :, left : left + width] = refs[index][:, source : source + width]
+
+    return pl.pallas_call(
+        kernel,
+        grid=(tok // step_rows,),
+        in_specs=[pl.BlockSpec((step_rows, array.shape[1]), lambda i: (i, 0)) for array in arrays],
+        out_specs=pl.BlockSpec((heads, step_rows, sum(widths)), lambda i: (0, i, 0)),
+        out_shape=jax.ShapeDtypeStruct((heads, tok, sum(widths)), arrays[0].dtype),
+        compiler_params=pltpu.CompilerParams(vmem_limit_bytes=VMEM),
+        name=name,
+    )(*arrays)
 
 
 def laid_out(received, planes, group):
     _, rows, features = received.shape
     if group == 1:
         return received.reshape(planes * rows, features)
-    routes = [
-        (
-            0,
-            (plane * group + local,),
-            (slice(plane * rows, (plane + 1) * rows), slice(local * features, (local + 1) * features)),
-        )
-        for plane in range(planes)
-        for local in range(group)
-    ]
-    return moved_blocks([received], (planes * rows, group * features), routes, "lay_out")
+
+    def kernel(blocks, out):
+        for local in range(group):
+            out[:, local * features : (local + 1) * features] = blocks[local]
+
+    return pl.pallas_call(
+        kernel,
+        grid=(planes,),
+        in_specs=[pl.BlockSpec((group, rows, features), lambda i: (i, 0, 0))],
+        out_specs=pl.BlockSpec((rows, group * features), lambda i: (i, 0)),
+        out_shape=jax.ShapeDtypeStruct((planes * rows, group * features), received.dtype),
+        compiler_params=pltpu.CompilerParams(vmem_limit_bytes=VMEM),
+        name="lay_out",
+    )(received)
 
 
 def solution(mesh):

time: 317 us -> 168 us (0.53)
  Pallas kernels: 190 us -> 36.9 us
    pallas_call x3, Pallas kernels: 162 us -> 5.28 us  [the longest x2 3.46 us: dealt(): pl.pallas_call(kernel, grid=(tok // step_rows,), in_specs=[pl.BlockSpec((...]
    all_gather x1, blocking collectives: 4.96 us -> 12.8 us  [per_device(): owner = lax.all_gather(piece_owner, 'local', axis=0, tiled=True)]
    all_to_all x1, blocking collectives: 80.6 us -> 75.9 us  [per_device(): lax.all_to_all(ordered, ('plane', 'local'), split_axis=0, concat_axis=0,...]
    pallas_call x1, Pallas kernels: 26.6 us -> 30.4 us  [attend(): pl.pallas_call(near_kernel, grid_spec=pltpu.PrefetchScalarGridSpec(num_sc...]
  transfers between devices with their start and end apart: 4 -> 4, of which waited for: 1 -> 1; matrix products, arithmetic and copies ran while one was open for 0% -> 0% of each run, Pallas kernels for 29% -> 19%
where the time goes in v1:
time: 168 us
  blocking collectives  88.7 us (53%)
  Pallas kernels  36.9 us (22%)
  waiting for transfers between devices  21.5 us (13%)
  starting transfers between devices  18.4 us (11%)
  local copies, waits for them, and re-layouts  2.24 us (1%)
    all_to_all x1, blocking collectives, per_device(): lax.all_to_all(ordered, ('plane', 'local'), split_axis=0, concat_axis=0,...  75.9 us
    pallas_call x1, Pallas kernels, attend(): pl.pallas_call(near_kernel, grid_spec=pltpu.PrefetchScalarGridSpec(num_sc...  30.4 us
    ppermute x2, waiting for transfers between devices, per_device(): moving = lax.ppermute(moving, 'plane', up)  21.5 us
    all_gather x1, blocking collectives, per_device(): owner = lax.all_gather(piece_owner, 'local', axis=0, tiled=True)  12.8 us
    ppermute x2, starting transfers between devices, per_device(): moving = lax.ppermute(moving, 'plane', up)  9.4 us
    all_to_all x2, starting transfers between devices, exchanged(): lax.all_to_all(split, ('local', 'head'), split_axis=0, concat_axis=0, til...  8.98 us
    pallas_call x2, Pallas kernels, dealt(): pl.pallas_call(kernel, grid=(tok // step_rows,), in_specs=[pl.BlockSpec((...  3.46 us
  transfers between devices with their start and end apart: 4, of which 1 were waited for; matrix products, arithmetic and copies ran while one was open for 0% of the time, Pallas kernels for 19%

profile of v1, /device:TPU:1, one launch (start us, length us, event | category | flops | bytes accessed | tf_op | source)
XLA Modules:
  0.0 167.8 jit_solution(17668852696871056546)
XLA Ops:
  0.0 0.0 copy-start
  0.0 0.0 copy-start.1
  0.0 1.2 copy-done.1
  1.2 0.0 copy-start.2
  1.2 1.0 copy-done.2
  2.2 1.6 deal_keys.1
  3.8 5.2 %all-to-all-start.1 = ((bf16[8,256,256]{2,1,0:T(8,128)(2,1)}), bf16[8,256,256]{2,1,0:T(8,128)(2,1)S(1)}, u32[]{:S(2)}, u32[]{:S(2)}) async-start(bf16[8,256,256]{2,1,0:T(8,128)(2,1)} %deal_keys.1), calls=%async_computation.1 | async-start | bytes 2097152 | tf_op jit(solution)/shard_map/all_to_all | solution.py:356
  9.1 0.0 copy-done
  9.1 0.0 copy-start.4
  9.1 1.9 %deal_queries.1 = bf16[8,256,512]{2,1,0:T(8,128)(2,1)} custom-call(bf16[256,4096]{1,0:T(8,128)(2,1)S(1)} %copy-done), custom_call_target="tpu_custom_call" | custom-call | tf_op jit(solution)/shard_map/deal_queries/pallas_call | solution.py:315
  10.9 0.0 copy-done.4
  10.9 12.8 %all-gather = s32[4,1,16]{2,1,0:T(1,128)S(1)} all-gather(s32[1,1,16]{2,1,0:T(1,128)S(1)} %bitcast.13), channel_id=1, replica_groups=mesh['plane'=4,'local'=4,'head'=2] {'local'}, dimensions={0}, use_global_device_ids=true | all-gather | bytes 320 | tf_op jit(solution)/shard_map/all_gather | solution.py:370
  23.8 0.0 copy-start.3
  23.8 0.0 all-to-all-done.1
  23.8 3.8 %all-to-all-start = ((bf16[8,256,512]{2,1,0:T(8,128)(2,1)}), bf16[8,256,512]{2,1,0:T(8,128)(2,1)S(1)}, u32[]{:S(2)}, u32[]{:S(2)}) async-start(bf16[8,256,512]{2,1,0:T(8,128)(2,1)} %deal_queries.1), calls=%async_computation | async-start | bytes 4194304 | tf_op jit(solution)/shard_map/all_to_all | solution.py:356
  27.5 4.2 %collective-permute-start = (bf16[2048,256]{1,0:T(8,128)(2,1)S(1)}, bf16[2048,256]{1,0:T(8,128)(2,1)}, u32[]{:S(2)}, u32[]{:S(2)}) collective-permute-start(bf16[2048,256]{1,0:T(8,128)(2,1)S(1)} %bitcast.9), channel_id=1, source_target_pairs={{0,8},{8,16},{16,24},{1,9},{9,17},{17,25},{2,10},{10,18},{18,26},{... | collective-permute-start | bytes 3145736 | tf_op jit(solution)/shard_map/ppermute | solution.py:368
  31.7 21.5 %collective-permute-done.near = bf16[2048,256]{1,0:T(8,128)(2,1)} collective-permute-done((bf16[2048,256]{1,0:T(8,128)(2,1)S(1)}, bf16[2048,256]{1,0:T(8,128)(2,1)}, u32[]{:S(2)}, u32[]{:S(2)}) %collective-permute-start) | collective-permute-done | bytes 1048608 | tf_op jit(solution)/shard_map/ppermute | solution.py:368
  53.2 5.2 %collective-permute-start.1 = (bf16[2048,256]{1,0:T(8,128)(2,1)}, bf16[2048,256]{1,0:T(8,128)(2,1)}, u32[]{:S(2)}, u32[]{:S(2)}) collective-permute-start(bf16[2048,256]{1,0:T(8,128)(2,1)} %collective-permute-done.near), channel_id=1, source_target_pairs={{0,8},{8,16},{16,24},{1,9},{9,17},{17,25},{2,10},{10,18},{18,26},{... | collective-permute-start | bytes 3145736 | tf_op jit(solution)/shard_map/ppermute | solution.py:368
  58.4 0.0 all-to-all-done
  58.4 0.0 copy-done.3
  58.4 30.4 %attend_near.1 = (bf16[16,4,32,512]{3,2,1,0:T(8,128)(2,1)S(1)}, f32[8,1024,128]{2,1,0:T(8,128)S(1)}, f32[8,1024,256]{2,1,0:T(8,128)S(1)}) custom-call(s32[1]{0:T(128)} %bitcast.at, s32[4]{0:T(128)S(1)} %copy-done.3, s32[4,16]{1,0:T(4,128)S(1)} %bitcast.11, bf16[2048,512]{1,0:T(8,128)(2,1)S(1)} %bitcast.6, bf16[2048,256]{1,0:T(8,128)(2,1)S(1)} %bitcast.10, ...), custom_call_target="tpu_custom_call" | custom-call | flops 20000000000 | bytes 8388608 | tf_op jit(solution)/shard_map/attend_near/pallas_call | solution.py:262
  88.8 0.0 collective-permute-done.1.refs_0_
  88.8 1.3 attend_far.1
  90.1 75.9 %all_to_all.15.blocks = bf16[16,128,512]{2,1,0:T(8,128)(2,1)S(1)} all-to-all(bf16[16,128,512]{2,1,0:T(8,128)(2,1)S(1)} %bitcast.8), channel_id=1, replica_groups=mesh['plane'=4,'local'=4,'head'=2] {'plane','local'}, dimensions={0} | all-to-all | bytes 4194304 | tf_op jit(solution)/shard_map/all_to_all | solution.py:378
  166.0 1.8 %lay_out.1 = bf16[512,2048]{1,0:T(8,128)(2,1)} custom-call(bf16[16,128,512]{2,1,0:T(8,128)(2,1)S(1)} %all_to_all.15.blocks), custom_call_target="tpu_custom_call" | custom-call | tf_op jit(solution)/shard_map/lay_out/pallas_call | solution.py:335
Async XLA Ops:
  0.0 9.1 %copy-start = (bf16[256,4096]{1,0:T(8,128)(2,1)S(1)}, bf16[256,4096]{1,0:T(8,128)(2,1)}, u32[]{:S(2)}) copy-start(bf16[256,4096]{1,0:T(8,128)(2,1)} %refs_0_.2) | copy-start | bytes 6291460
  0.0 1.2 copy-start.1
  1.2 1.0 copy-start.2
  3.8 19.9 %all-to-all-start.1 = ((bf16[8,256,256]{2,1,0:T(8,128)(2,1)}), bf16[8,256,256]{2,1,0:T(8,128)(2,1)S(1)}, u32[]{:S(2)}, u32[]{:S(2)}) async-start(bf16[8,256,256]{2,1,0:T(8,128)(2,1)} %deal_keys.1), calls=%async_computation.1 | async-start | bytes 2097152 | tf_op jit(solution)/shard_map/all_to_all | solution.py:356
  9.1 1.9 %copy-start.4 = (s32[1,16]{1,0:T(1,128)S(1)}, s32[1,16]{1,0:T(1,128)}, u32[]{:S(2)}) copy-start(s32[1,16]{1,0:T(1,128)} %param.9) | copy-start | bytes 196
  23.8 34.7 %copy-start.3 = (s32[4]{0:T(128)S(1)}, s32[4]{0:T(128)}, u32[]{:S(2)}) copy-start(s32[4]{0:T(128)} %lengths.3) | copy-start | bytes 52
  23.8 34.7 %all-to-all-start = ((bf16[8,256,512]{2,1,0:T(8,128)(2,1)}), bf16[8,256,512]{2,1,0:T(8,128)(2,1)S(1)}, u32[]{:S(2)}, u32[]{:S(2)}) async-start(bf16[8,256,512]{2,1,0:T(8,128)(2,1)} %deal_queries.1), calls=%async_computation | async-start | bytes 4194304 | tf_op jit(solution)/shard_map/all_to_all | solution.py:356
  27.5 25.7 %collective-permute-start = (bf16[2048,256]{1,0:T(8,128)(2,1)S(1)}, bf16[2048,256]{1,0:T(8,128)(2,1)}, u32[]{:S(2)}, u32[]{:S(2)}) collective-permute-start(bf16[2048,256]{1,0:T(8,128)(2,1)S(1)} %bitcast.9), channel_id=1, source_target_pairs={{0,8},{8,16},{16,24},{1,9},{9,17},{17,25},{2,10},{10,18},{18,26},{... | collective-permute-start | bytes 3145736 | tf_op jit(solution)/shard_map/ppermute | solution.py:368
  53.2 35.6 %collective-permute-start.1 = (bf16[2048,256]{1,0:T(8,128)(2,1)}, bf16[2048,256]{1,0:T(8,128)(2,1)}, u32[]{:S(2)}, u32[]{:S(2)}) collective-permute-start(bf16[2048,256]{1,0:T(8,128)(2,1)} %collective-permute-done.near), channel_id=1, source_target_pairs={{0,8},{8,16},{16,24},{1,9},{9,17},{17,25},{2,10},{10,18},{18,26},{... | collective-permute-start | bytes 3145736 | tf_op jit(solution)/shard_map/ppermute | solution.py:368

commit v2 on v1

--- a/solution.py
+++ b/solution.py
@@ -17,6 +17,7 @@
 MASKED = -1e30
 SCALE = math.log2(math.e) / math.sqrt(HD)
 VMEM = 32 * 1024 * 1024
+VMEM_FIRST = 60 * 1024 * 1024
 
 
 def doc_start(place, ends):
@@ -27,10 +28,10 @@
 
 
 class Block:
-    def __init__(self, ends, first_row, base, window, turned, values, qs, top, total):
+    def __init__(self, ends, first_row, base, pairs, qs, top, total):
         self.ends = ends
-        self.first_row, self.base, self.window = first_row, base, window
-        self.turned, self.values, self.qs, self.top, self.total = turned, values, qs, top, total
+        self.first_row, self.base, self.window = first_row, base, pairs.shape[0]
+        self.pairs, self.qs, self.top, self.total = pairs, qs, top, total
         self.first_start = doc_start(first_row, self.ends) - base
         self.last_start = doc_start(first_row + Q_ROWS - 1, self.ends) - base
 
@@ -44,9 +45,9 @@
 
     def run(self, at, size, masked):
         at = pl.multiple_of(at, K_SHORT)
-        keys = self.turned[:, pl.ds(at, size)]
-        keys = jnp.concatenate([keys, keys], axis=0)
-        values = self.values[pl.ds(at, size), :]
+        values = self.pairs[pl.ds(at, size), :HD]
+        keys = self.pairs[pl.ds(at, size), HD:]
+        keys = jnp.concatenate([keys, keys], axis=1)
         values = jnp.concatenate([values, jnp.ones_like(values)], axis=1)
         if masked:
             shape = (Q_ROWS, size)
@@ -56,7 +57,9 @@
 
         def score(head):
             rows = slice(head * Q_ROWS, (head + 1) * Q_ROWS)
-            return jnp.dot(self.qs[rows], keys, preferred_element_type=jnp.float32)
+            return lax.dot_general(
+                self.qs[rows], keys, (((1,), (1,)), ((), ())), preferred_element_type=jnp.float32
+            )
 
         scores = score(0)
         for head in range(QPK):
@@ -76,7 +79,8 @@
     def cover(self, high, long):
         low = jnp.clip(self.first_start, 0, self.window) // K_SHORT * K_SHORT
         plain = (jnp.clip(self.last_start, 0, self.window) + K_SHORT - 1) // K_SHORT * K_SHORT
-        for size, masked, until in ((long, False, plain), (long, True, low), (K_SHORT, True, low)):
+        middle = max(long // 2, K_SHORT)
+        for size, masked, until in ((long, False, plain), (long, True, low), (middle, True, low), (K_SHORT, True, low)):
             count = jnp.maximum(high - until, 0) // size
             lax.fori_loop(
                 0,
@@ -101,19 +105,6 @@
     return pltpu.make_async_copy(stage.at[slot], out.at[owner[slot // out.shape[0], slot % out.shape[0]], slot // out.shape[0]], sems.at[slot])
 
 
-def arrange(refs, turned, values):
-    tokens = refs[0].shape[0]
-    for index, ref in enumerate(refs):
-        values[index * tokens : (index + 1) * tokens] = ref[:, :HD]
-
-        def turn(tile, carry, ref=ref, index=index):
-            rows = pl.ds(pl.multiple_of(tile * HD, HD), HD)
-            turned[:, pl.ds(pl.multiple_of(index * tokens + tile * HD, HD), HD)] = ref[rows, HD:].T
-            return carry
-
-        lax.fori_loop(0, tokens // HD, turn, 0)
-
-
 def keep(step, slot, top, total, tops, totals, kept, back):
     pairs = ((top.at[slot], tops.at[step]), (total.at[slot], totals.at[step]))
     if back:
@@ -135,7 +126,7 @@
     return ends
 
 
-def near_kernel(at, lengths, owner, q_ref, own, near, out, tops, totals, turned, values, qs, top, total, stage, sems, kept):
+def near_kernel(at, lengths, owner, q_ref, own, near, out, tops, totals, pairs, qs, top, total, stage, sems, kept, brought):
     tokens = own.shape[0]
     step = pl.program_id(0)
     slot = lax.rem(step, 2)
@@ -146,7 +137,14 @@
 
     @pl.when(step == 0)
     def _():
-        arrange((near, own), turned, values)
+        copies = [
+            pltpu.make_async_copy(ref, pairs.at[index * tokens : (index + 1) * tokens], brought.at[index])
+            for index, ref in enumerate((near, own))
+        ]
+        for copy in copies:
+            copy.start()
+        for copy in copies:
+            copy.wait()
 
     @pl.when((step >= 2) & (step - 2 < needed))
     def _():
@@ -154,7 +152,7 @@
             copy.wait()
 
     first_row = place + step * Q_ROWS
-    block = Block(ends, first_row, place - tokens, 2 * tokens, turned, values, qs, top.at[slot], total.at[slot])
+    block = Block(ends, first_row, place - tokens, pairs, qs, top.at[slot], total.at[slot])
     block.load(q_ref)
     top[slot] = jnp.full(top.shape[1:], MASKED, jnp.float32)
     total[slot] = jnp.zeros(total.shape[1:], jnp.float32)
@@ -191,7 +189,7 @@
 
 
 def far_kernel(at, lengths, owner, q_rows, tops, totals, begun, *refs):
-    far, (out, held, fetched, turned, values, qs, top, total, stage, sems, kept, brought) = refs[:-12], refs[-12:]
+    far, (out, held, pairs, qs, top, total, stage, sems, kept, brought) = refs[:-10], refs[-10:]
     del begun
     tokens = q_rows.shape[0]
     window = tokens * len(far)
@@ -206,12 +204,14 @@
 
     @pl.when(needed > 0)
     def _():
-        whole = [pltpu.make_async_copy(ref, fetched.at[index], brought.at[index]) for index, ref in enumerate(far[::-1])]
+        whole = [
+            pltpu.make_async_copy(ref, pairs.at[index * tokens : (index + 1) * tokens], brought.at[index])
+            for index, ref in enumerate(far[::-1])
+        ]
         for copy in whole + coming(0, 0):
             copy.start()
         for copy in whole:
             copy.wait()
-        arrange([fetched.at[index] for index in range(len(far))], turned, values)
 
     def one(step, carry):
         slot = lax.rem(step, 2)
@@ -222,7 +222,7 @@
                 copy.start()
 
         first_row = place + step * Q_ROWS
-        block = Block(ends, first_row, place - tokens - window, window, turned, values, qs, top.at[slot], total.at[slot])
+        block = Block(ends, first_row, place - tokens - window, pairs, qs, top.at[slot], total.at[slot])
         for copy in coming(step, slot):
             copy.wait()
         block.load(held.at[slot])
@@ -240,7 +240,6 @@
     near, far = steps_back[0], steps_back[1:]
     rows = QPK * Q_ROWS
     any_spec = pl.BlockSpec(memory_space=pl.ANY)
-    paired_spec = pl.BlockSpec(own.shape, lambda i, *_: (0, 0))
     out_shape = jax.ShapeDtypeStruct((n_owner, tokens // (n_owner * piece), piece, features), jnp.bfloat16)
     state_shapes = [
         jax.ShapeDtypeStruct((blocks, rows, HD), jnp.float32),
@@ -249,14 +248,14 @@
 
     def scratch(window):
         return [
-            pltpu.VMEM((HD, window), jnp.bfloat16),
-            pltpu.VMEM((window, HD), jnp.bfloat16),
+            pltpu.VMEM((window, 2 * HD), jnp.bfloat16),
             pltpu.VMEM((rows, 2 * HD), jnp.bfloat16),
             pltpu.VMEM((2, rows, HD), jnp.float32),
             pltpu.VMEM((2, rows, 2 * HD), jnp.float32),
             pltpu.VMEM((tokens // piece, piece, features), jnp.bfloat16),
             pltpu.SemaphoreType.DMA((tokens // piece,)),
             pltpu.SemaphoreType.DMA((2, 3)),
+            pltpu.SemaphoreType.DMA((window // tokens,)),
         ]
 
     begun, tops, totals = pl.pallas_call(
@@ -264,7 +263,7 @@
         grid_spec=pltpu.PrefetchScalarGridSpec(
             num_scalar_prefetch=3,
             grid=(blocks,),
-            in_specs=[pl.BlockSpec((Q_ROWS, features), lambda i, *_: (i, 0)), paired_spec, paired_spec],
+            in_specs=[pl.BlockSpec((Q_ROWS, features), lambda i, *_: (i, 0)), any_spec, any_spec],
             out_specs=[any_spec] * 3,
             scratch_shapes=scratch(2 * tokens),
         ),
@@ -284,9 +283,7 @@
             out_specs=any_spec,
             scratch_shapes=[
                 pltpu.VMEM((2, Q_ROWS, features), jnp.bfloat16),
-                pltpu.VMEM((len(far),) + own.shape, jnp.bfloat16),
                 *scratch(tokens * len(far)),
-                pltpu.SemaphoreType.DMA((len(far),)),
             ],
         ),
         out_shape=out_shape,
@@ -318,7 +315,7 @@
         in_specs=[pl.BlockSpec((step_rows, array.shape[1]), lambda i: (i, 0)) for array in arrays],
         out_specs=pl.BlockSpec((heads, step_rows, sum(widths)), lambda i: (0, i, 0)),
         out_shape=jax.ShapeDtypeStruct((heads, tok, sum(widths)), arrays[0].dtype),
-        compiler_params=pltpu.CompilerParams(vmem_limit_bytes=VMEM),
+        compiler_params=pltpu.CompilerParams(vmem_limit_bytes=VMEM_FIRST),
         name=name,
     )(*arrays)
 

time: 168 us -> 169 us (level)
  blocking collectives: 88.7 us -> 92.3 us
  local copies, waits for them, and re-layouts: 2.24 us -> 0.01 us
    pallas_call x1, Pallas kernels: 30.4 us -> 24.8 us  [attend(): pl.pallas_call(near_kernel, grid_spec=pltpu.PrefetchScalarGridSpec(num_sc...]
    all_to_all x1, blocking collectives: 75.9 us -> 81.4 us  [per_device(): lax.all_to_all(ordered, ('plane', 'local'), split_axis=0, concat_axis=0,...]
    pallas_call x2, Pallas kernels: 3.46 us -> 7.26 us  [dealt(): pl.pallas_call(kernel, grid=(tok // step_rows,), in_specs=[pl.BlockSpec((...]
    unnamed x10 -> x4, local copies, waits for them, and re-layouts: 2.24 us -> 0.01 us
    all_gather x1, blocking collectives: 12.8 us -> 10.9 us  [per_device(): owner = lax.all_gather(piece_owner, 'local', axis=0, tiled=True)]
  transfers between devices with their start and end apart: 4 -> 4, of which waited for: 1 -> 1; matrix products, arithmetic and copies ran while one was open for 0% -> 0% of each run, Pallas kernels for 19% -> 17%
where the time goes in v2:
time: 169 us; the launch traced here: 168 us
  blocking collectives  92.3 us (55%)
  Pallas kernels  35.4 us (21%)
  waiting for transfers between devices  21.5 us (13%)
  starting transfers between devices  18.4 us (11%)
    all_to_all x1, blocking collectives, per_device(): lax.all_to_all(ordered, ('plane', 'local'), split_axis=0, concat_axis=0,...  81.4 us
    pallas_call x1, Pallas kernels, attend(): pl.pallas_call(near_kernel, grid_spec=pltpu.PrefetchScalarGridSpec(num_sc...  24.8 us
    ppermute x2, waiting for transfers between devices, per_device(): moving = lax.ppermute(moving, 'plane', up)  21.5 us
    all_gather x1, blocking collectives, per_device(): owner = lax.all_gather(piece_owner, 'local', axis=0, tiled=True)  10.9 us
    ppermute x2, starting transfers between devices, per_device(): moving = lax.ppermute(moving, 'plane', up)  9.43 us
    all_to_all x2, starting transfers between devices, exchanged(): lax.all_to_all(split, ('local', 'head'), split_axis=0, concat_axis=0, til...  8.98 us
    pallas_call x2, Pallas kernels, dealt(): pl.pallas_call(kernel, grid=(tok // step_rows,), in_specs=[pl.BlockSpec((...  7.26 us
  transfers between devices with their start and end apart: 4, of which 1 were waited for; matrix products, arithmetic and copies ran while one was open for 0% of the time, Pallas kernels for 17%

profile of v2, /device:TPU:1, one launch (start us, length us, event | category | flops | bytes accessed | tf_op | source)
XLA Modules:
  0.0 167.7 jit_solution(15101226461914991404)
XLA Ops:
  0.0 3.5 %deal_keys.1 = bf16[8,256,256]{2,1,0:T(8,128)(2,1)} custom-call(bf16[256,1024]{1,0:T(8,128)(2,1)} %refs_0_.3, bf16[256,1024]{1,0:T(8,128)(2,1)} %refs_1_.1), custom_call_target="tpu_custom_call" | custom-call | tf_op jit(solution)/shard_map/deal_keys/pallas_call | solution.py:312
  3.5 5.2 %all-to-all-start.1 = ((bf16[8,256,256]{2,1,0:T(8,128)(2,1)}), bf16[8,256,256]{2,1,0:T(8,128)(2,1)S(1)}, u32[]{:S(2)}, u32[]{:S(2)}) async-start(bf16[8,256,256]{2,1,0:T(8,128)(2,1)} %deal_keys.1), calls=%async_computation.1 | async-start | bytes 2097152 | tf_op jit(solution)/shard_map/all_to_all | solution.py:353
  8.7 0.0 copy-start.1
  8.7 3.8 %deal_queries.1 = bf16[8,256,512]{2,1,0:T(8,128)(2,1)} custom-call(bf16[256,4096]{1,0:T(8,128)(2,1)} %refs_0_.2), custom_call_target="tpu_custom_call" | custom-call | tf_op jit(solution)/shard_map/deal_queries/pallas_call | solution.py:312
  12.5 0.0 copy-done.1
  12.5 10.9 %all-gather = s32[4,1,16]{2,1,0:T(1,128)S(1)} all-gather(s32[1,1,16]{2,1,0:T(1,128)S(1)} %bitcast.13), channel_id=1, replica_groups=mesh['plane'=4,'local'=4,'head'=2] {'local'}, dimensions={0}, use_global_device_ids=true | all-gather | bytes 320 | tf_op jit(solution)/shard_map/all_gather | solution.py:367
  23.4 0.0 copy-start
  23.4 0.0 all-to-all-done.1
  23.4 3.8 %all-to-all-start = ((bf16[8,256,512]{2,1,0:T(8,128)(2,1)}), bf16[8,256,512]{2,1,0:T(8,128)(2,1)S(1)}, u32[]{:S(2)}, u32[]{:S(2)}) async-start(bf16[8,256,512]{2,1,0:T(8,128)(2,1)} %deal_queries.1), calls=%async_computation | async-start | bytes 4194304 | tf_op jit(solution)/shard_map/all_to_all | solution.py:353
  27.2 4.2 %collective-permute-start = (bf16[2048,256]{1,0:T(8,128)(2,1)S(1)}, bf16[2048,256]{1,0:T(8,128)(2,1)}, u32[]{:S(2)}, u32[]{:S(2)}) collective-permute-start(bf16[2048,256]{1,0:T(8,128)(2,1)S(1)} %bitcast.9), channel_id=1, source_target_pairs={{0,8},{8,16},{16,24},{1,9},{9,17},{17,25},{2,10},{10,18},{18,26},{... | collective-permute-start | bytes 3145736 | tf_op jit(solution)/shard_map/ppermute | solution.py:365
  31.3 21.5 %collective-permute-done.near = bf16[2048,256]{1,0:T(8,128)(2,1)} collective-permute-done((bf16[2048,256]{1,0:T(8,128)(2,1)S(1)}, bf16[2048,256]{1,0:T(8,128)(2,1)}, u32[]{:S(2)}, u32[]{:S(2)}) %collective-permute-start) | collective-permute-done | bytes 1048608 | tf_op jit(solution)/shard_map/ppermute | solution.py:365
  52.9 5.2 %collective-permute-start.1 = (bf16[2048,256]{1,0:T(8,128)(2,1)}, bf16[2048,256]{1,0:T(8,128)(2,1)}, u32[]{:S(2)}, u32[]{:S(2)}) collective-permute-start(bf16[2048,256]{1,0:T(8,128)(2,1)} %collective-permute-done.near), channel_id=1, source_target_pairs={{0,8},{8,16},{16,24},{1,9},{9,17},{17,25},{2,10},{10,18},{18,26},{... | collective-permute-start | bytes 3145736 | tf_op jit(solution)/shard_map/ppermute | solution.py:365
  58.1 0.0 all-to-all-done
  58.1 0.0 copy-done
  58.1 24.8 %attend_near.1 = (bf16[16,4,32,512]{3,2,1,0:T(8,128)(2,1)S(1)}, f32[8,1024,128]{2,1,0:T(8,128)S(1)}, f32[8,1024,256]{2,1,0:T(8,128)S(1)}) custom-call(s32[1]{0:T(128)} %bitcast.at, s32[4]{0:T(128)S(1)} %copy-done, s32[4,16]{1,0:T(4,128)S(1)} %bitcast.11, bf16[2048,512]{1,0:T(8,128)(2,1)S(1)} %bitcast.6, bf16[2048,256]{1,0:T(8,128)(2,1)S(1)} %bitcast.10, ...), custom_call_target="tpu_custom_call" | custom-call | flops 20000000000 | bytes 8388608 | tf_op jit(solution)/shard_map/attend_near/pallas_call | solution.py:261
  82.9 0.0 collective-permute-done.1.refs_0_
  82.9 1.5 attend_far.1
  84.4 81.4 %all_to_all.15.blocks = bf16[16,128,512]{2,1,0:T(8,128)(2,1)S(1)} all-to-all(bf16[16,128,512]{2,1,0:T(8,128)(2,1)S(1)} %bitcast.8), channel_id=1, replica_groups=mesh['plane'=4,'local'=4,'head'=2] {'plane','local'}, dimensions={0} | all-to-all | bytes 4194304 | tf_op jit(solution)/shard_map/all_to_all | solution.py:375
  165.8 1.8 %lay_out.1 = bf16[512,2048]{1,0:T(8,128)(2,1)} custom-call(bf16[16,128,512]{2,1,0:T(8,128)(2,1)S(1)} %all_to_all.15.blocks), custom_call_target="tpu_custom_call" | custom-call | tf_op jit(solution)/shard_map/lay_out/pallas_call | solution.py:332
Async XLA Ops:
  3.5 19.9 %all-to-all-start.1 = ((bf16[8,256,256]{2,1,0:T(8,128)(2,1)}), bf16[8,256,256]{2,1,0:T(8,128)(2,1)S(1)}, u32[]{:S(2)}, u32[]{:S(2)}) async-start(bf16[8,256,256]{2,1,0:T(8,128)(2,1)} %deal_keys.1), calls=%async_computation.1 | async-start | bytes 2097152 | tf_op jit(solution)/shard_map/all_to_all | solution.py:353
  8.7 3.8 %copy-start.1 = (s32[1,16]{1,0:T(1,128)S(1)}, s32[1,16]{1,0:T(1,128)}, u32[]{:S(2)}) copy-start(s32[1,16]{1,0:T(1,128)} %param.9) | copy-start | bytes 196
  23.4 34.7 %copy-start = (s32[4]{0:T(128)S(1)}, s32[4]{0:T(128)}, u32[]{:S(2)}) copy-start(s32[4]{0:T(128)} %lengths.3) | copy-start | bytes 52
  23.4 34.7 %all-to-all-start = ((bf16[8,256,512]{2,1,0:T(8,128)(2,1)}), bf16[8,256,512]{2,1,0:T(8,128)(2,1)S(1)}, u32[]{:S(2)}, u32[]{:S(2)}) async-start(bf16[8,256,512]{2,1,0:T(8,128)(2,1)} %deal_queries.1), calls=%async_computation | async-start | bytes 4194304 | tf_op jit(solution)/shard_map/all_to_all | solution.py:353
  27.2 25.7 %collective-permute-start = (bf16[2048,256]{1,0:T(8,128)(2,1)S(1)}, bf16[2048,256]{1,0:T(8,128)(2,1)}, u32[]{:S(2)}, u32[]{:S(2)}) collective-permute-start(bf16[2048,256]{1,0:T(8,128)(2,1)S(1)} %bitcast.9), channel_id=1, source_target_pairs={{0,8},{8,16},{16,24},{1,9},{9,17},{17,25},{2,10},{10,18},{18,26},{... | collective-permute-start | bytes 3145736 | tf_op jit(solution)/shard_map/ppermute | solution.py:365
  52.9 30.1 %collective-permute-start.1 = (bf16[2048,256]{1,0:T(8,128)(2,1)}, bf16[2048,256]{1,0:T(8,128)(2,1)}, u32[]{:S(2)}, u32[]{:S(2)}) collective-permute-start(bf16[2048,256]{1,0:T(8,128)(2,1)} %collective-permute-done.near), channel_id=1, source_target_pairs={{0,8},{8,16},{16,24},{1,9},{9,17},{17,25},{2,10},{10,18},{18,26},{... | collective-permute-start | bytes 3145736 | tf_op jit(solution)/shard_map/ppermute | solution.py:365
